TPU v7x, 256 devices: a whole 4x4x8 slice. The times are simulated.
256 devices in a mesh: seq: 64 (over z, x, core), head: 4 (over y).
Axes of the slice: x: 4, y: 4, z: 8, core: 2. Of those that a mesh axis runs over, the one named last changes fastest.
Arguments:
- queries: bfloat16 [32768, 4096], P(('seq', 'head')), may hold values from -6 to 6
- keys: bfloat16 [32768, 4096], P(('seq', 'head')), may hold values from -6 to 6
- values: bfloat16 [32768, 4096], P(('seq', 'head')), may hold values from -6 to 6
- grad_out: bfloat16 [32768, 4096], P(('seq', 'head')), may hold values from -0.0029296875 to 0.0029296875
Outputs:
- grad_queries: bfloat16 [32768, 4096], P(('seq', 'head'))
- grad_keys: bfloat16 [32768, 4096], P(('seq', 'head'))
- grad_values: bfloat16 [32768, 4096], P(('seq', 'head'))
All inputs are finite; a program needn't handle non-finite values.
Results may differ from a plain program's by a relative error of at most 0.005.
Values may be sent and summed in bfloat16 or wider, within the bound.
A program may use at most 256 MiB of HBM per device.

v0:
```python
import jax
import jax.numpy as jnp
from jax import lax
from jax.sharding import PartitionSpec as P

H = 32
DH = 128


def carried_in(value, axis, join, neutral, backward):
    count, mine = (lax.axis_size(axis), lax.axis_index(axis))
    pieces = lax.all_gather(value, axis)
    if backward:
        pieces = pieces[::-1]
        mine = count - 1 - mine
    subtotal = jnp.full_like(value, 0) + jnp.asarray(neutral, value.dtype)

    def turn(position, subtotal):
        longer = join(subtotal, pieces[position])
        return jnp.where(position < mine, longer, subtotal)

    return lax.fori_loop(0, count - 1, turn, subtotal)


def add_states(earlier, later):
    return earlier + later


def batched(left, right, left_dim, right_dim):
    return lax.dot_general(
        left, right, (((left_dim,), (right_dim,)), ((0,), (0,))), preferred_element_type=jnp.float32
    )


def heads_first(array):
    return jnp.swapaxes(array, 0, 1)


def shards(queries, keys, values, grad_out):
    tokens_here = queries.shape[0]
    split_queries = queries.reshape(tokens_here, H, DH)
    split_keys = keys.reshape(tokens_here, H, DH)
    split_values = values.reshape(tokens_here, H, DH)
    split_grads = grad_out.reshape(tokens_here, H, DH)
    head_queries, head_keys, head_values, head_grads = (
        lax.all_to_all(split_queries, "head", split_axis=1, concat_axis=0, tiled=True),
        lax.all_to_all(split_keys, "head", split_axis=1, concat_axis=0, tiled=True),
        lax.all_to_all(split_values, "head", split_axis=1, concat_axis=0, tiled=True),
        lax.all_to_all(split_grads, "head", split_axis=1, concat_axis=0, tiled=True),
    )
    key_state = jnp.einsum(
        "shd,she->hde", head_keys, head_values, preferred_element_type=jnp.float32
    )
    grad_state = jnp.einsum(
        "thd,the->hde", head_queries, head_grads, preferred_element_type=jnp.float32
    )
    empty_state = jnp.zeros_like(key_state)
    prefix = carried_in(key_state, "seq", add_states, empty_state, False)
    suffix = carried_in(grad_state, "seq", add_states, empty_state, True)
    prefix_low = prefix.astype(jnp.bfloat16)
    suffix_low = suffix.astype(jnp.bfloat16)
    lead_queries = heads_first(head_queries)
    lead_keys = heads_first(head_keys)
    lead_values = heads_first(head_values)
    lead_grads = heads_first(head_grads)
    length = lead_queries.shape[1]
    row_index = lax.broadcasted_iota(jnp.int32, (length, length), 0)
    column_index = lax.broadcasted_iota(jnp.int32, (length, length), 1)
    causal = (column_index <= row_index)[None]
    grad_scores = jnp.where(causal, batched(lead_grads, lead_values, 2, 2), 0.0).astype(
        jnp.bfloat16
    )
    query_scores = jnp.where(causal, batched(lead_queries, lead_keys, 2, 2), 0.0).astype(
        jnp.bfloat16
    )
    grad_queries = batched(
        jnp.concatenate([grad_scores, lead_grads], axis=2),
        jnp.concatenate([lead_keys, jnp.swapaxes(prefix_low, 1, 2)], axis=1),
        2,
        1,
    )
    grad_keys = batched(
        jnp.concatenate([jnp.swapaxes(grad_scores, 1, 2), lead_values], axis=2),
        jnp.concatenate([lead_queries, jnp.swapaxes(suffix_low, 1, 2)], axis=1),
        2,
        1,
    )
    grad_values = batched(
        jnp.concatenate([jnp.swapaxes(query_scores, 1, 2), lead_keys], axis=2),
        jnp.concatenate([lead_grads, suffix_low], axis=1),
        2,
        1,
    )
    back_queries, back_keys, back_values = (
        lax.all_to_all(
            heads_first(grad_queries.astype(jnp.bfloat16)),
            "head",
            split_axis=0,
            concat_axis=1,
            tiled=True,
        ),
        lax.all_to_all(
            heads_first(grad_keys.astype(jnp.bfloat16)),
            "head",
            split_axis=0,
            concat_axis=1,
            tiled=True,
        ),
        lax.all_to_all(
            heads_first(grad_values.astype(jnp.bfloat16)),
            "head",
            split_axis=0,
            concat_axis=1,
            tiled=True,
        ),
    )
    return (
        back_queries.reshape(tokens_here, H * DH),
        back_keys.reshape(tokens_here, H * DH),
        back_values.reshape(tokens_here, H * DH),
    )


def solution(mesh):
    return jax.shard_map(
        shards,
        mesh=mesh,
        in_specs=(
            P(("seq", "head"), None),
            P(("seq", "head"), None),
            P(("seq", "head"), None),
            P(("seq", "head"), None),
        ),
        out_specs=(P(("seq", "head"), None), P(("seq", "head"), None), P(("seq", "head"), None)),
        check_vma=False,
    )
```

profile of v0, /device:TPU:1, one launch (start us, length us, event | category | flops | bytes accessed | tf_op | source)
XLA Modules:
  0.0 450.1 jit_solution(375447117454986203)
XLA Ops:
  7.2 1.7 copy.76
  8.9 1.3 copy.77
  10.2 5.0 %all-to-all-start.4 = ((bf16[128,32,128]{2,0,1:T(8,128)(2,1)}), bf16[128,32,128]{2,0,1:T(8,128)(2,1)S(1)}, u32[]{:S(2)}, u32[]{:S(2)}) async-start(bf16[128,32,128]{2,0,1:T(8,128)(2,1)} %copy.77), calls=%async_computation.4 | async-start | bytes 2097152 | tf_op jit(solution)/shard_map/all_to_all | solution.py:46
  15.9 1.3 copy.58
  17.2 11.4 %all-to-all-done.4 = bf16[128,32,128]{2,0,1:T(8,128)(2,1)S(1)} async-done(((bf16[128,32,128]{2,0,1:T(8,128)(2,1)}), bf16[128,32,128]{2,0,1:T(8,128)(2,1)S(1)}, u32[]{:S(2)}, u32[]{:S(2)}) %all-to-all-start.4) | async-done | bytes 1048608 | tf_op jit(solution)/shard_map/all_to_all | solution.py:46
  28.6 3.5 all-to-all-start
  33.4 10.9 %all-to-all-done = bf16[128,32,128]{2,0,1:T(8,128)(2,1)S(1)} async-done(((bf16[128,32,128]{2,0,1:T(8,128)(2,1)}), bf16[128,32,128]{2,0,1:T(8,128)(2,1)S(1)}, u32[]{:S(2)}, u32[]{:S(2)}) %all-to-all-start) | async-done | bytes 1048608 | tf_op jit(solution)/shard_map/all_to_all | solution.py:49
  45.7 1.6 copy.67
  47.3 1.3 copy.68
  48.6 3.5 all-to-all-start.2
  52.2 1.6 copy.61
  53.8 1.3 copy.62
  55.1 8.0 %all-to-all-done.2 = bf16[128,32,128]{2,0,1:T(8,128)(2,1)S(1)} async-done(((bf16[128,32,128]{2,0,1:T(8,128)(2,1)}), bf16[128,32,128]{2,0,1:T(8,128)(2,1)S(1)}, u32[]{:S(2)}, u32[]{:S(2)}) %all-to-all-start.2) | async-done | bytes 1048608 | tf_op jit(solution)/shard_map/all_to_all | solution.py:47
  63.1 3.5 all-to-all-start.1
  66.7 1.4 copy.70
  68.1 1.5 all_to_all.96
  69.6 6.8 %all-to-all-done.1 = bf16[128,32,128]{2,0,1:T(8,128)(2,1)S(1)} async-done(((bf16[128,32,128]{2,0,1:T(8,128)(2,1)}), bf16[128,32,128]{2,0,1:T(8,128)(2,1)S(1)}, u32[]{:S(2)}, u32[]{:S(2)}) %all-to-all-start.1) | async-done | bytes 1048608 | tf_op jit(solution)/shard_map/all_to_all | solution.py:48
  77.4 1.3 copy.64
  80.1 4.6 %fusion = (bf16[8,512,512]{1,2,0:T(8,128)(2,1)}, bf16[8,512,512]{2,1,0:T(8,128)(2,1)}) fusion(pred[512,512]{0,1:T(8,128)(4,1)S(1)} %iota_compare_fusion, bf16[8,512,128]{2,1,0:T(8,128)(2,1)S(1)} %bitcast.86, bf16[8,512,128]{2,1,0:T(8,128)(2,1)S(1)} %bitcast.90), kind=kOutput, calls=%fused_computation.3 | convolution fusion | flops 538968064 | bytes 10747904 | tf_op jit(solution)/shard_map/dot_general | solution.py:30
  84.8 6.5 %copy.65 = bf16[8,512,512]{1,2,0:T(8,128)(2,1)} copy(bf16[8,512,512]{2,1,0:T(8,128)(2,1)} %get-tuple-element.210) | data formatting | bytes 8388608 | tf_op jit(solution)/shard_map/dot_general | solution.py:30
  91.3 4.9 %select_convert_fusion = bf16[8,512,512]{1,2,0:T(8,128)(2,1)} fusion(pred[512,512]{0,1:T(8,128)(4,1)} %copy-done.7, bf16[512,8,128]{0,2,1:T(8,128)(2,1)} %copy-done.2, bf16[512,8,128]{0,2,1:T(8,128)(2,1)} %copy-done), kind=kOutput, calls=%fused_computation.4 | convolution fusion | flops 541065216 | bytes 6553600 | tf_op jit(solution)/shard_map/dot_general | solution.py:30
  96.1 97.5 %all-gather.7.cloned.1.call-done = f32[512,128,128]{2,1,0:T(8,128)} async-done(((f32[8,128,128]{2,1,0:T(8,128)}), f32[512,128,128]{2,1,0:T(8,128)}) %all-gather.7.cloned.1.call-update) | async-done | bytes 33554448 | tf_op jit(solution)/shard_map/all_gather | solution.py:12
  193.6 23.2 %rev.3 = f32[64,8,128,128]{3,2,1,0:T(8,128)} reverse(f32[64,8,128,128]{3,2,1,0:T(8,128)} %bitcast.84), dimensions={0} | reverse | bytes 67108864 | tf_op jit(solution)/shard_map/rev | solution.py:14
  216.8 79.9 %while.29 = (s32[]{:T(128)}, f32[8,128,128]{2,1,0:T(8,128)S(1)}, s32[]{:T(128)}, f32[64,8,128,128]{3,2,1,0:T(8,128)}, s32[]{:T(128)}, /*index=5*/s32[]{:T(128)}) while((s32[]{:T(128)}, f32[8,128,128]{2,1,0:T(8,128)S(1)}, s32[]{:T(128)}, f32[64,8,128,128]{3,2,1,0:T(8,128)}, s32[]{:T(128)}, /*index=5*/s32[]{:T(128)}) %tuple.68), condition=%wide.region_3.4_spmd.clone, body=%wide.region_2.3_spmd.clone.sunk | while | flops 393220 | bytes 1572965 | solution.py:22
  218.1 1.3 add_select_fusion.5
  219.4 1.2 add_select_fusion.5
  221.9 1.2 add_select_fusion.5
  247.0 1.4 add_select_fusion.5
  248.4 1.3 add_select_fusion.5
  253.5 1.3 add_select_fusion.5
  256.1 1.3 add_select_fusion.5
  257.4 1.3 add_select_fusion.5
  262.4 1.3 add_select_fusion.5
  263.7 1.2 add_select_fusion.5
  267.4 1.3 add_select_fusion.5
  268.7 1.2 add_select_fusion.5
  272.5 1.3 add_select_fusion.5
  273.8 1.3 add_select_fusion.5
  280.2 1.3 add_select_fusion.5
  281.5 1.2 add_select_fusion.5
  282.7 1.2 add_select_fusion.5
  284.0 1.3 add_select_fusion.5
  285.3 1.3 add_select_fusion.5
  290.4 1.3 add_select_fusion.5
  295.4 1.3 add_select_fusion.5
  296.8 4.3 fusion.28
  301.1 1.6 copy.87
  302.7 4.5 all-to-all-start.6
  307.2 5.4 %select_convert_fusion.1 = bf16[8,512,512]{1,2,0:T(8,128)(2,1)} fusion(bf16[8,512,512]{1,2,0:T(8,128)(2,1)} %copy.65, pred[512,512]{0,1:T(8,128)(4,1)S(1)} %iota_compare_fusion.1), kind=kLoop, calls=%fused_computation.5 | loop fusion | flops 2097152 | bytes 8650752 | tf_op jit(solution)/shard_map/convert_element_type | solution.py:70
  312.6 1.3 copy.75
  313.9 1.3 copy.66
  315.2 4.5 fusion.25
  319.7 1.6 copy.82
  321.9 3.5 all-to-all-start.5
  325.4 10.5 %all-gather.5.cloned.1.call-done = f32[512,128,128]{2,1,0:T(8,128)} async-done(((f32[8,128,128]{2,1,0:T(8,128)}), f32[512,128,128]{2,1,0:T(8,128)}) %all-gather.5.cloned.1.call-update) | async-done | bytes 33554448 | tf_op jit(solution)/shard_map/all_gather | solution.py:12
  335.9 78.9 %while.28 = (s32[]{:T(128)}, f32[8,128,128]{2,1,0:T(8,128)S(1)}, s32[]{:T(128)}, f32[64,8,128,128]{3,2,1,0:T(8,128)}, s32[]{:T(128)}, /*index=5*/s32[]{:T(128)}) while((s32[]{:T(128)}, f32[8,128,128]{2,1,0:T(8,128)S(1)}, s32[]{:T(128)}, f32[64,8,128,128]{3,2,1,0:T(8,128)}, s32[]{:T(128)}, /*index=5*/s32[]{:T(128)}) %tuple.75), condition=%wide.region_1.2_spmd.clone, body=%wide.region_0.1_spmd.clone.sunk | while | flops 393220 | bytes 1572965 | solution.py:22
  335.9 1.3 add_select_fusion.4
  414.9 4.2 fusion.22
  419.1 1.6 copy.73
  420.7 4.0 all-to-all-start.3
  424.7 2.4 copy.88
  428.3 11.1 %all-to-all-done.3 = bf16[512,8,128]{2,1,0:T(8,128)(2,1)S(1)} async-done(((bf16[512,8,128]{2,1,0:T(8,128)(2,1)}), bf16[512,8,128]{2,1,0:T(8,128)(2,1)S(1)}, u32[]{:S(2)}, u32[]{:S(2)}) %all-to-all-start.3) | async-done | bytes 1048608 | tf_op jit(solution)/shard_map/all_to_all | solution.py:95
  439.6 1.4 copy.106
  441.0 2.2 copy_bitcast_fusion
  (141 shorter events, 135.3 us)
Async XLA Ops:
  7.2 8.0 %copy-start.6 = (bf16[128,4096]{1,0:T(8,128)(2,1)S(1)}, bf16[128,4096]{1,0:T(8,128)(2,1)}, u32[]{:S(2)}) copy-start(bf16[128,4096]{1,0:T(8,128)(2,1)} %param.11) | copy-start | bytes 3145732
  10.2 18.4 %all-to-all-start.4 = ((bf16[128,32,128]{2,0,1:T(8,128)(2,1)}), bf16[128,32,128]{2,0,1:T(8,128)(2,1)S(1)}, u32[]{:S(2)}, u32[]{:S(2)}) async-start(bf16[128,32,128]{2,0,1:T(8,128)(2,1)} %copy.77), calls=%async_computation.4 | async-start | bytes 2097152 | tf_op jit(solution)/shard_map/all_to_all | solution.py:46
  28.6 15.7 %all-to-all-start = ((bf16[128,32,128]{2,0,1:T(8,128)(2,1)}), bf16[128,32,128]{2,0,1:T(8,128)(2,1)S(1)}, u32[]{:S(2)}, u32[]{:S(2)}) async-start(bf16[128,32,128]{2,0,1:T(8,128)(2,1)} %copy.58), calls=%async_computation | async-start | bytes 2097152 | tf_op jit(solution)/shard_map/all_to_all | solution.py:49
  32.1 161.5 %all-gather.7.cloned.1.call-start = ((), (), s32[]{:S(2)}) async-start(), calls=%async_computation.8 | async-start | bytes 34078720 | tf_op jit(solution)/shard_map/all_gather | solution.py:12
  33.4 15.2 %copy-start.2 = (bf16[512,8,128]{0,2,1:T(8,128)(2,1)}, bf16[512,8,128]{0,2,1:T(8,128)(2,1)S(1)}, u32[]{:S(2)}) copy-start(bf16[512,8,128]{0,2,1:T(8,128)(2,1)S(1)} %all_to_all.103) | copy-start | bytes 3145732
  48.6 14.5 %all-to-all-start.2 = ((bf16[128,32,128]{2,0,1:T(8,128)(2,1)}), bf16[128,32,128]{2,0,1:T(8,128)(2,1)S(1)}, u32[]{:S(2)}, u32[]{:S(2)}) async-start(bf16[128,32,128]{2,0,1:T(8,128)(2,1)} %copy.68), calls=%async_computation.2 | async-start | bytes 2097152 | tf_op jit(solution)/shard_map/all_to_all | solution.py:47
  63.1 13.3 %all-to-all-start.1 = ((bf16[128,32,128]{2,0,1:T(8,128)(2,1)}), bf16[128,32,128]{2,0,1:T(8,128)(2,1)S(1)}, u32[]{:S(2)}, u32[]{:S(2)}) async-start(bf16[128,32,128]{2,0,1:T(8,128)(2,1)} %copy.62), calls=%async_computation.1 | async-start | bytes 2097152 | tf_op jit(solution)/shard_map/all_to_all | solution.py:48
  66.6 269.3 %all-gather.5.cloned.1.call-start = ((), (), s32[]{:S(2)}) async-start(), calls=%async_computation.7 | async-start | bytes 34078720 | tf_op jit(solution)/shard_map/all_gather | solution.py:12
  69.6 10.3 %copy-start = (bf16[512,8,128]{0,2,1:T(8,128)(2,1)}, bf16[512,8,128]{0,2,1:T(8,128)(2,1)S(1)}, u32[]{:S(2)}) copy-start(bf16[512,8,128]{0,2,1:T(8,128)(2,1)S(1)} %all_to_all.96) | copy-start | bytes 3145732
  76.4 1.0 copy-start.3
  80.0 4.7 %copy-start.7 = (pred[512,512]{0,1:T(8,128)(4,1)}, pred[512,512]{0,1:T(8,128)(4,1)S(1)}, u32[]{:S(2)}) copy-start(pred[512,512]{0,1:T(8,128)(4,1)S(1)} %iota_compare_fusion) | copy-start | bytes 786436
  302.7 19.1 %all-to-all-start.6 = ((bf16[512,8,128]{2,1,0:T(8,128)(2,1)}), bf16[512,8,128]{2,1,0:T(8,128)(2,1)}, u32[]{:S(2)}, u32[]{:S(2)}) async-start(bf16[512,8,128]{2,1,0:T(8,128)(2,1)} %copy.87), calls=%async_computation.6 | async-start | bytes 2097152 | tf_op jit(solution)/shard_map/all_to_all | solution.py:109
  321.9 98.9 %all-to-all-start.5 = ((bf16[512,8,128]{2,1,0:T(8,128)(2,1)}), bf16[512,8,128]{2,1,0:T(8,128)(2,1)S(1)}, u32[]{:S(2)}, u32[]{:S(2)}) async-start(bf16[512,8,128]{2,1,0:T(8,128)(2,1)} %copy.82), calls=%async_computation.5 | async-start | bytes 2097152 | tf_op jit(solution)/shard_map/all_to_all | solution.py:102
  335.9 78.9 %copy-start.1 = (bf16[512,8,128]{0,2,1:T(8,128)(2,1)S(1)}, bf16[512,8,128]{0,2,1:T(8,128)(2,1)}, u32[]{:S(2)}) copy-start(bf16[512,8,128]{0,2,1:T(8,128)(2,1)} %copy-done) | copy-start | bytes 3145732
  420.7 18.7 %all-to-all-start.3 = ((bf16[512,8,128]{2,1,0:T(8,128)(2,1)}), bf16[512,8,128]{2,1,0:T(8,128)(2,1)S(1)}, u32[]{:S(2)}, u32[]{:S(2)}) async-start(bf16[512,8,128]{2,1,0:T(8,128)(2,1)} %copy.73), calls=%async_computation.3 | async-start | bytes 2097152 | tf_op jit(solution)/shard_map/all_to_all | solution.py:95
  428.3 12.7 %copy-start.4 = (bf16[128,4,8,128]{3,2,1,0:T(8,128)(2,1)S(1)}, bf16[128,4,8,128]{3,2,1,0:T(8,128)(2,1)}, u32[]{:S(2)}) copy-start(bf16[128,4,8,128]{3,2,1,0:T(8,128)(2,1)} %copy.88) | copy-start | bytes 3145732
  428.3 12.7 %copy-start.5 = (bf16[128,4,8,128]{3,2,1,0:T(8,128)(2,1)S(1)}, bf16[128,4,8,128]{3,2,1,0:T(8,128)(2,1)}, u32[]{:S(2)}) copy-start(bf16[128,4,8,128]{3,2,1,0:T(8,128)(2,1)} %copy.83) | copy-start | bytes 3145732
Sparse Core Ops, SparseCore 0:
  45.8 147.7 all-gather.6
  196.4 139.4 all-gather.4
where the time goes:
time: 457 us; the launch traced here: 450 us
  other arithmetic  161 us (35%)
  waiting for transfers between devices  157 us (34%)
  local copies, waits for them, and re-layouts  61.9 us (14%)
  starting transfers between devices  27.6 us (6%)
  matrix products  25 us (5%)
  between operations  14.3 us (3%)
    select_n x126, other arithmetic, turn(): return jnp.where(position < mine, longer, subtotal)  156 us
    all_gather x2, waiting for transfers between devices, carried_in(): pieces = lax.all_gather(value, axis)  108 us
    rev x1, local copies, waits for them, and re-layouts, carried_in(): pieces = pieces[::-1]  23.2 us
    dot_general x5, matrix products, batched(): lax.dot_general(left, right, (((left_dim,), (right_dim,)), ((0,), (0,))),...  22.5 us
    all_to_all x1, waiting for transfers between devices, shards(): lax.all_to_all(split_queries, 'head', split_axis=1, concat_axis=0, tiled=...  11.4 us
    all_to_all x1, waiting for transfers between devices, shards(): lax.all_to_all(heads_first(grad_queries.astype(jnp.bfloat16)), 'head', sp...  11.1 us
    all_to_all x1, waiting for transfers between devices, shards(): lax.all_to_all(split_grads, 'head', split_axis=1, concat_axis=0, tiled=True)  10.9 us
  transfers between devices with their start and end apart: 9, of which 8 were waited for; matrix products, arithmetic and copies ran while one was open for 53% of the time, Pallas kernels for 0%

commit v1 on v0

v1 whole, which is shorter than its diff:
```python
import jax
import jax.numpy as jnp
from jax import lax
from jax.experimental import pallas as pl
from jax.experimental.pallas import tpu as pltpu
from jax.sharding import PartitionSpec as P

H = 32
DH = 128
NZ, NX, NY = 8, 4, 4
PER = H // NY
M = 4
HC = PER // M
R = HC * DH
RX = R // NX
MESH = pl.DeviceIdType.MESH
F32 = jnp.float32
BF16 = jnp.bfloat16


def dot(left, right, left_dim, right_dim):
    return lax.dot_general(
        left, right, (((left_dim,), (right_dim,)), ((), ())), preferred_element_type=F32
    )


def kernel(
    q_ref, k_ref, v_ref, g_ref, oq_ref, ok_ref, ov_ref,
    sent, got, own_total, other_total, core_out, x_out, x_in, z_buf, x_back, base, base_out, base_other,
    y_out, final, part_q, part_k, part_v,
    yi_s, yi_r, c1_s, c1_r, xi_s, xi_r, zz_s, zz_r, xo_s, xo_r, c2_s, c2_r, yo_s, yo_r,
):
    s = lax.axis_index("seq")
    y = lax.axis_index("head")
    c = lax.rem(s, 2)
    x = lax.rem(s // 2, NX)
    z = s // (2 * NX)
    forward = c == 0
    mate = (s + 1 - 2 * c, y)

    def at_y(d):
        return lax.rem(y + d, NY)

    def at_x(d):
        return lax.rem(x + d, NX)

    def at_z(d):
        return lax.rem(z + d, NZ)

    def x_dev(i):
        return ((z * NX + i) * 2 + c, y)

    def z_dev(i):
        return ((i * NX + x) * 2 + c, y)

    def copy(src, dst, send, recv, device):
        return pltpu.make_async_remote_copy(
            src_ref=src, dst_ref=dst, send_sem=send, recv_sem=recv, device_id=device, device_id_type=MESH
        )

    barrier = pltpu.get_barrier_semaphore()
    partners = (
        [mate]
        + [(s, at_y(d)) for d in range(1, NY)]
        + [x_dev(at_x(d)) for d in range(1, NX)]
        + [z_dev(at_z(d)) for d in range(1, NZ)]
    )
    for partner in partners:
        pl.semaphore_signal(barrier, inc=1, device_id=partner, device_id_type=MESH)

    def lanes(head):
        return pl.ds(pl.multiple_of(head * DH, DH), DH)

    def y_in(m, d, receive=False):
        slot = at_y(NY - d) if receive else y
        return copy(sent.at[m, at_y(d)], got.at[m, slot], yi_s.at[m, d], yi_r.at[m, d], (s, at_y(d)))

    def core_in(m):
        return copy(core_out.at[m], other_total.at[m], c1_s.at[m], c1_r.at[m], mate)

    def x_in_copy(m, d, receive=False):
        slot = at_x(NX - d) if receive else x
        return copy(x_out.at[m, at_x(d)], x_in.at[m, slot], xi_s.at[m, d], xi_r.at[m, d], x_dev(at_x(d)))

    def z_copy(m, d, receive=False):
        slot = at_z(NZ - d) if receive else z
        return copy(z_buf.at[m, z], z_buf.at[m, slot], zz_s.at[m, d], zz_r.at[m, d], z_dev(at_z(d)))

    def x_out_copy(m, d, receive=False):
        slot = at_x(NX - d) if receive else x
        return copy(x_back.at[m, at_x(d)], base.at[m, slot], xo_s.at[m, d], xo_r.at[m, d], x_dev(at_x(d)))

    def core_out_copy(m):
        return copy(base_out.at[m], base_other.at[m], c2_s.at[m], c2_r.at[m], mate)

    def y_out_copy(m, d, receive=False):
        slot = at_y(NY - d) if receive else y
        return copy(y_out.at[m, at_y(d)], final.at[m, slot], yo_s.at[m, d], yo_r.at[m, d], (s, at_y(d)))

    def states(m):
        for d in (2, 1, 3, 0):
            owner = at_y(d)

            @pl.loop(0, HC)
            def _(i):
                at = lanes(owner * PER + m * HC + i)
                rows = pl.ds(pl.multiple_of(i * DH, DH), DH)
                key_state = dot(k_ref[:, at], v_ref[:, at], 0, 0).astype(BF16)
                grad_state = dot(q_ref[:, at], g_ref[:, at], 0, 0).astype(BF16)
                if d:
                    sent[m, owner, 0, rows, :] = key_state
                    sent[m, owner, 1, rows, :] = grad_state
                else:
                    got[m, y, 0, rows, :] = key_state
                    got[m, y, 1, rows, :] = grad_state

            if d:
                y_in(m, d).start()

    def inside(m):
        row = lax.broadcasted_iota(jnp.int32, (DH, DH), 0)
        column = lax.broadcasted_iota(jnp.int32, (DH, DH), 1)
        causal = column <= row

        @pl.loop(0, NY * HC)
        def _(n):
            at = lanes(n // HC * PER + m * HC + lax.rem(n, HC))
            q, k, v, g = q_ref[:, at], k_ref[:, at], v_ref[:, at], g_ref[:, at]
            grad_scores = jnp.where(causal, dot(g, v, 1, 1), 0.0).astype(BF16)
            query_scores = jnp.where(causal, dot(q, k, 1, 1), 0.0).astype(BF16)
            part_q[:, at] = dot(grad_scores, k, 1, 0)
            part_k[:, at] = dot(grad_scores, q, 0, 0)
            part_v[:, at] = dot(query_scores, g, 0, 0)

    def stage_c(m):
        for d in range(1, NY):
            y_in(m, d, True).wait_recv()

        @pl.loop(0, HC)
        def _(i):
            rows = pl.ds(pl.multiple_of(i * DH, DH), DH)
            totals = []
            for kind in range(2):
                total = got[m, 0, kind, rows, :].astype(F32)
                for j in range(1, NY):
                    total += got[m, j, kind, rows, :].astype(F32)
                totals.append(total)
            own_total[m, rows, :] = jnp.where(forward, totals[0], totals[1])
            core_out[m, rows, :] = jnp.where(forward, totals[1], totals[0])

        core_in(m).start()

    def stage_d(m):
        core_in(m).wait_recv()
        for i in range(NX):
            rows = slice(i * RX, (i + 1) * RX)
            x_out[m, i] = own_total[m, rows, :] + other_total[m, rows, :]
        for d in range(1, NX):
            x_in_copy(m, d).start()
        x_in[m, x] = x_out[m, x]

    def stage_e(m):
        for d in range(1, NX):
            x_in_copy(m, d, True).wait_recv()
        total = x_in[m, 0]
        for i in range(1, NX):
            total += x_in[m, i]
        z_buf[m, z] = total.astype(BF16)
        for d in range(1, NZ):
            z_copy(m, d).start()

    def stage_z(m):
        for d in range(1, NZ):
            z_copy(m, d, True).wait_recv()
        before = jnp.zeros((RX, DH), F32)
        for i in range(NZ):
            wanted = jnp.where(forward, i < z, i > z)
            before += jnp.where(wanted, z_buf[m, i].astype(F32), 0.0)
        ahead = [before]
        behind = [before]
        for i in range(NX - 1):
            ahead.append(ahead[-1] + x_in[m, i])
            behind.append(behind[-1] + x_in[m, NX - 1 - i])
        for i in range(NX):
            x_back[m, i] = jnp.where(forward, ahead[i], behind[NX - 1 - i])
        for d in range(1, NX):
            x_out_copy(m, d).start()
        base[m, x] = x_back[m, x]

    def stage_f(m):
        for d in range(1, NX):
            x_out_copy(m, d, True).wait_recv()
        for i in range(NX):
            rows = slice(i * RX, (i + 1) * RX)
            base_out[m, rows, :] = base[m, i] + own_total[m, rows, :]
        core_out_copy(m).start()

    def stage_g(m):
        core_out_copy(m).wait_recv()
        for i in range(NX):
            rows = slice(i * RX, (i + 1) * RX)
            mine = base[m, i]
            theirs = base_other[m, rows, :]
            run = jnp.where(forward, mine, theirs)
            for j in range(NY):
                y_out[m, j, 0, rows, :] = run.astype(BF16)
                if j < NY - 1:
                    run += got[m, j, 0, rows, :].astype(F32)
            run = jnp.where(forward, theirs, mine)
            for j in range(NY - 1, -1, -1):
                y_out[m, j, 1, rows, :] = run.astype(BF16)
                if j:
                    run += got[m, j, 1, rows, :].astype(F32)
        for d in (2, 1, 3):
            y_out_copy(m, d).start()
        final[m, y] = y_out[m, y]

    def stage_h(m):
        for d in range(1, NY):
            y_out_copy(m, d, True).wait_recv()

        @pl.loop(0, NY * HC)
        def _(n):
            owner, i = n // HC, lax.rem(n, HC)
            at = lanes(owner * PER + m * HC + i)
            rows = pl.ds(pl.multiple_of(i * DH, DH), DH)
            prefix = final[m, owner, 0, rows, :]
            suffix = final[m, owner, 1, rows, :]
            oq_ref[:, at] = (part_q[:, at] + dot(g_ref[:, at], prefix, 1, 1)).astype(BF16)
            ok_ref[:, at] = (part_k[:, at] + dot(v_ref[:, at], suffix, 1, 1)).astype(BF16)
            ov_ref[:, at] = (part_v[:, at] + dot(k_ref[:, at], suffix, 1, 0)).astype(BF16)

    pl.semaphore_wait(barrier, len(partners))
    for m in range(M):
        states(m)
    for m in range(M):
        inside(m)
    stage_c(0)
    stage_d(0)
    stage_e(0)
    for m in range(M):
        stage_z(m)
        if m + 1 < M:
            stage_c(m + 1)
        stage_f(m)
        if m + 1 < M:
            stage_d(m + 1)
        stage_g(m)
        if m + 1 < M:
            stage_e(m + 1)
    for m in range(M):
        stage_h(m)
    for m in range(M):
        for d in range(1, NY):
            y_in(m, d).wait_send()
            y_out_copy(m, d).wait_send()
        for d in range(1, NX):
            x_in_copy(m, d).wait_send()
            x_out_copy(m, d).wait_send()
        for d in range(1, NZ):
            z_copy(m, d).wait_send()
        core_in(m).wait_send()
        core_out_copy(m).wait_send()


def shards(queries, keys, values, grad_out):
    tokens = queries.shape[0]
    whole = pl.BlockSpec(memory_space=pltpu.VMEM)
    dma = pltpu.SemaphoreType.DMA
    return pl.pallas_call(
        kernel,
        out_shape=[jax.ShapeDtypeStruct((tokens, H * DH), BF16)] * 3,
        in_specs=[whole] * 4,
        out_specs=[whole] * 3,
        scratch_shapes=[
            pltpu.VMEM((M, NY, 2, R, DH), BF16),
            pltpu.VMEM((M, NY, 2, R, DH), BF16),
            pltpu.VMEM((M, R, DH), F32),
            pltpu.VMEM((M, R, DH), F32),
            pltpu.VMEM((M, R, DH), F32),
            pltpu.VMEM((M, NX, RX, DH), F32),
            pltpu.VMEM((M, NX, RX, DH), F32),
            pltpu.VMEM((M, NZ, RX, DH), BF16),
            pltpu.VMEM((M, NX, RX, DH), F32),
            pltpu.VMEM((M, NX, RX, DH), F32),
            pltpu.VMEM((M, R, DH), F32),
            pltpu.VMEM((M, R, DH), F32),
            pltpu.VMEM((M, NY, 2, R, DH), BF16),
            pltpu.VMEM((M, NY, 2, R, DH), BF16),
            pltpu.VMEM((tokens, H * DH), F32),
            pltpu.VMEM((tokens, H * DH), F32),
            pltpu.VMEM((tokens, H * DH), F32),
            dma((M, NY)), dma((M, NY)),
            dma((M,)), dma((M,)),
            dma((M, NX)), dma((M, NX)),
            dma((M, NZ)), dma((M, NZ)),
            dma((M, NX)), dma((M, NX)),
            dma((M,)), dma((M,)),
            dma((M, NY)), dma((M, NY)),
        ],
        compiler_params=pltpu.CompilerParams(
            collective_id=0, has_side_effects=True, vmem_limit_bytes=48 * 2**20
        ),
        cost_estimate=pl.CostEstimate(
            flops=20 * DH**3 * H, bytes_accessed=14 * tokens * H * DH, transcendentals=0
        ),
        name="scan",
    )(queries, keys, values, grad_out)


def solution(mesh):
    spec = P(("seq", "head"), None)
    return jax.shard_map(
        shards, mesh=mesh, in_specs=(spec,) * 4, out_specs=(spec,) * 3, check_vma=False
    )
```

time: 457 us -> 106 us (0.23); the launches traced: 450 us -> 106 us
  other arithmetic: 161 us -> 0 us
  waiting for transfers between devices: 157 us -> 0 us
  Pallas kernels: 0 us -> 99.9 us
  local copies, waits for them, and re-layouts: 61.9 us -> 5.35 us
  starting transfers between devices: 27.6 us -> 0 us
  matrix products: 25 us -> 0 us
  between operations: 14.3 us -> 0.65 us
    select_n x126 -> x0, other arithmetic: 156 us -> none  [turn(): return jnp.where(position < mine, longer, subtotal)]
    all_gather x2 -> x0, waiting for transfers between devices: 108 us -> none  [carried_in(): pieces = lax.all_gather(value, axis)]
    pallas_call x0 -> x1, Pallas kernels: none -> 99.9 us  [shards(): pl.pallas_call(kernel, out_shape=[jax.ShapeDtypeStruct((tokens, H * DH),...]
    all_to_all x7 -> x0, waiting for transfers between devices: 48.8 us -> none  [the longest x1 11.4 us: shards(): lax.all_to_all(split_queries, 'head', split_axis=1, concat_axis=0, tiled=...]
    all_to_all x7 -> x0, starting transfers between devices: 27.6 us -> none  [the longest x1 5.01 us: shards(): lax.all_to_all(split_queries, 'head', split_axis=1, concat_axis=0, tiled=...]
    dot_general x7 -> x0, matrix products: 25 us -> none  [the longest x5 22.5 us: batched(): lax.dot_general(left, right, (((left_dim,), (right_dim,)), ((0,), (0,))),...]
    rev x1 -> x0, local copies, waits for them, and re-layouts: 23.2 us -> none  [carried_in(): pieces = pieces[::-1]]
    all_to_all x9 -> x0, local copies, waits for them, and re-layouts: 9.18 us -> none  [the longest x2 2.9 us: shards(): lax.all_to_all(split_keys, 'head', split_axis=1, concat_axis=0, tiled=True)]
  transfers between devices with their start and end apart: 9 -> 0, of which waited for: 8 -> 0; matrix products, arithmetic and copies ran while one was open for 53% -> 0% of each run, Pallas kernels for 0% -> 0%
where the time goes in v1:
time: 106 us
  Pallas kernels  99.9 us (94%)
  local copies, waits for them, and re-layouts  5.35 us (5%)
    pallas_call x1, Pallas kernels, shards(): pl.pallas_call(kernel, out_shape=[jax.ShapeDtypeStruct((tokens, H * DH),...  99.9 us
    unnamed x7, local copies, waits for them, and re-layouts  5.35 us

profile of v1, /device:TPU:1, one launch (start us, length us, event | category | flops | bytes accessed | tf_op | source)
XLA Modules:
  0.0 105.9 jit_solution(11093504982343734752)
XLA Ops:
  0.6 0.0 copy-start
  0.6 1.2 %copy-done = bf16[128,4096]{1,0:T(8,128)(2,1)S(1)} copy-done((bf16[128,4096]{1,0:T(8,128)(2,1)S(1)}, bf16[128,4096]{1,0:T(8,128)(2,1)}, u32[]{:S(2)}) %copy-start) | copy-done | bytes 1048600
  1.9 0.0 copy-start.1
  1.9 1.2 %copy-done.1 = bf16[128,4096]{1,0:T(8,128)(2,1)S(1)} copy-done((bf16[128,4096]{1,0:T(8,128)(2,1)S(1)}, bf16[128,4096]{1,0:T(8,128)(2,1)}, u32[]{:S(2)}) %copy-start.1) | copy-done | bytes 1048600
  3.1 99.9 %scan.1 = (bf16[128,4096]{1,0:T(8,128)(2,1)S(1)}, bf16[128,4096]{1,0:T(8,128)(2,1)S(1)}, bf16[128,4096]{1,0:T(8,128)(2,1)S(1)}) custom-call(bf16[128,4096]{1,0:T(8,128)(2,1)S(1)} %copy-done, bf16[128,4096]{1,0:T(8,128)(2,1)S(1)} %copy-done.1, bf16[128,4096]{1,0:T(8,128)(2,1)} %v_ref.1, bf16[128,4096]{1,0:T(8,128)(2,1)} %g_ref.1), custom_call_target="tpu_custom_call" | custom-call | flops 1342177280 | bytes 7340032 | tf_op jit(solution)/shard_map/scan/pallas_call | solution.py:270
  103.0 1.0 copy.10
  103.9 1.0 copy.11
  104.9 1.0 copy.12
Async XLA Ops:
  0.6 1.2 %copy-start = (bf16[128,4096]{1,0:T(8,128)(2,1)S(1)}, bf16[128,4096]{1,0:T(8,128)(2,1)}, u32[]{:S(2)}) copy-start(bf16[128,4096]{1,0:T(8,128)(2,1)} %q_ref.1) | copy-start | bytes 3145732
  1.9 1.2 %copy-start.1 = (bf16[128,4096]{1,0:T(8,128)(2,1)S(1)}, bf16[128,4096]{1,0:T(8,128)(2,1)}, u32[]{:S(2)}) copy-start(bf16[128,4096]{1,0:T(8,128)(2,1)} %k_ref.1) | copy-start | bytes 3145732

commit v2 on v1

--- a/solution.py
+++ b/solution.py
@@ -11,8 +11,10 @@
 PER = H // NY
 M = 4
 HC = PER // M
+WIDE = NY * HC * DH
 R = HC * DH
 RX = R // NX
+UNROLL = 4
 MESH = pl.DeviceIdType.MESH
 F32 = jnp.float32
 BF16 = jnp.bfloat16
@@ -25,10 +27,10 @@
 
 
 def kernel(
-    q_ref, k_ref, v_ref, g_ref, oq_ref, ok_ref, ov_ref,
-    sent, got, own_total, other_total, core_out, x_out, x_in, z_buf, x_back, base, base_out, base_other,
+    q_hbm, k_hbm, v_hbm, g_hbm, oq_hbm, ok_hbm, ov_hbm,
+    q_ref, k_ref, v_ref, g_ref, oq_ref, ok_ref, ov_ref, sent, got, own_total, other_total, core_out, x_out, x_in, z_buf, x_back, base, base_out, base_other,
     y_out, final, part_q, part_k, part_v,
-    yi_s, yi_r, c1_s, c1_r, xi_s, xi_r, zz_s, zz_r, xo_s, xo_r, c2_s, c2_r, yo_s, yo_r,
+    in_sem, out_sem, yi_s, yi_r, c1_s, c1_r, xi_s, xi_r, zz_s, zz_r, xo_s, xo_r, c2_s, c2_r, yo_s, yo_r,
 ):
     s = lax.axis_index("seq")
     y = lax.axis_index("head")
@@ -68,8 +70,28 @@
     for partner in partners:
         pl.semaphore_signal(barrier, inc=1, device_id=partner, device_id_type=MESH)
 
-    def lanes(head):
-        return pl.ds(pl.multiple_of(head * DH, DH), DH)
+    def lanes(m, owner, i):
+        return pl.ds(pl.multiple_of(((m * NY + owner) * HC + i) * DH, DH), DH)
+
+    def load(m):
+        columns = slice(m * WIDE, (m + 1) * WIDE)
+        pairs = ((k_hbm, k_ref), (v_hbm, v_ref), (q_hbm, q_ref), (g_hbm, g_ref))
+        return [
+            pltpu.make_async_copy(a.at[:, columns], b.at[:, columns], in_sem.at[m, n])
+            for n, (a, b) in enumerate(pairs)
+        ]
+
+    def store(m):
+        columns = slice(m * WIDE, (m + 1) * WIDE)
+        pairs = ((oq_ref, oq_hbm), (ok_ref, ok_hbm), (ov_ref, ov_hbm))
+        return [
+            pltpu.make_async_copy(a.at[:, columns], b.at[:, columns], out_sem.at[m, n])
+            for n, (a, b) in enumerate(pairs)
+        ]
+
+    for m in range(M):
+        for one in load(m):
+            one.start()
 
     def y_in(m, d, receive=False):
         slot = at_y(NY - d) if receive else y
@@ -98,13 +120,13 @@
         return copy(y_out.at[m, at_y(d)], final.at[m, slot], yo_s.at[m, d], yo_r.at[m, d], (s, at_y(d)))
 
     def states(m):
+        for one in load(m):
+            one.wait()
         for d in (2, 1, 3, 0):
             owner = at_y(d)
-
-            @pl.loop(0, HC)
-            def _(i):
-                at = lanes(owner * PER + m * HC + i)
-                rows = pl.ds(pl.multiple_of(i * DH, DH), DH)
+            for i in range(HC):
+                at = lanes(m, owner, i)
+                rows = slice(i * DH, (i + 1) * DH)
                 key_state = dot(k_ref[:, at], v_ref[:, at], 0, 0).astype(BF16)
                 grad_state = dot(q_ref[:, at], g_ref[:, at], 0, 0).astype(BF16)
                 if d:
@@ -113,7 +135,6 @@
                 else:
                     got[m, y, 0, rows, :] = key_state
                     got[m, y, 1, rows, :] = grad_state
-
             if d:
                 y_in(m, d).start()
 
@@ -122,15 +143,16 @@
         column = lax.broadcasted_iota(jnp.int32, (DH, DH), 1)
         causal = column <= row
 
-        @pl.loop(0, NY * HC)
+        @pl.loop(0, NY * HC // UNROLL)
         def _(n):
-            at = lanes(n // HC * PER + m * HC + lax.rem(n, HC))
-            q, k, v, g = q_ref[:, at], k_ref[:, at], v_ref[:, at], g_ref[:, at]
-            grad_scores = jnp.where(causal, dot(g, v, 1, 1), 0.0).astype(BF16)
-            query_scores = jnp.where(causal, dot(q, k, 1, 1), 0.0).astype(BF16)
-            part_q[:, at] = dot(grad_scores, k, 1, 0)
-            part_k[:, at] = dot(grad_scores, q, 0, 0)
-            part_v[:, at] = dot(query_scores, g, 0, 0)
+            for u in range(UNROLL):
+                at = lanes(m, 0, n * UNROLL + u)
+                q, k, v, g = q_ref[:, at], k_ref[:, at], v_ref[:, at], g_ref[:, at]
+                grad_scores = jnp.where(causal, dot(g, v, 1, 1), 0.0).astype(BF16)
+                query_scores = jnp.where(causal, dot(q, k, 1, 1), 0.0).astype(BF16)
+                part_q[:, at] = dot(grad_scores, k, 1, 0)
+                part_k[:, at] = dot(grad_scores, q, 0, 0)
+                part_v[:, at] = dot(query_scores, g, 0, 0)
 
     def stage_c(m):
         for d in range(1, NY):
@@ -219,38 +241,36 @@
         for d in range(1, NY):
             y_out_copy(m, d, True).wait_recv()
 
-        @pl.loop(0, NY * HC)
+        @pl.loop(0, NY * HC // UNROLL)
         def _(n):
-            owner, i = n // HC, lax.rem(n, HC)
-            at = lanes(owner * PER + m * HC + i)
-            rows = pl.ds(pl.multiple_of(i * DH, DH), DH)
-            prefix = final[m, owner, 0, rows, :]
-            suffix = final[m, owner, 1, rows, :]
-            oq_ref[:, at] = (part_q[:, at] + dot(g_ref[:, at], prefix, 1, 1)).astype(BF16)
-            ok_ref[:, at] = (part_k[:, at] + dot(v_ref[:, at], suffix, 1, 1)).astype(BF16)
-            ov_ref[:, at] = (part_v[:, at] + dot(k_ref[:, at], suffix, 1, 0)).astype(BF16)
-
+            for u in range(UNROLL):
+                owner, i = (n * UNROLL + u) // HC, lax.rem(n * UNROLL + u, HC)
+                at = lanes(m, owner, i)
+                rows = pl.ds(pl.multiple_of(i * DH, DH), DH)
+                prefix = final[m, owner, 0, rows, :]
+                suffix = final[m, owner, 1, rows, :]
+                oq_ref[:, at] = (part_q[:, at] + dot(g_ref[:, at], prefix, 1, 1)).astype(BF16)
+                ok_ref[:, at] = (part_k[:, at] + dot(v_ref[:, at], suffix, 1, 1)).astype(BF16)
+                ov_ref[:, at] = (part_v[:, at] + dot(k_ref[:, at], suffix, 1, 0)).astype(BF16)
+
+        for one in store(m):
+            one.start()
+
+    steps = []
+    for m in range(M):
+        arrives = 23.0 * (m + 1) / M
+        after = ((stage_c, 0), (stage_d, 1.2), (stage_e, 4.2), (stage_z, 9.5), (stage_f, 13), (stage_g, 14))
+        steps += [(arrives + t, m, stage) for stage, t in after]
+        steps.append((arrives + 23, m, stage_h))
+        steps.append((2.0 + 2.5 * m, m, inside))
     pl.semaphore_wait(barrier, len(partners))
     for m in range(M):
         states(m)
+    for _, m, stage in sorted(steps, key=lambda step: step[:2]):
+        stage(m)
     for m in range(M):
-        inside(m)
-    stage_c(0)
-    stage_d(0)
-    stage_e(0)
-    for m in range(M):
-        stage_z(m)
-        if m + 1 < M:
-            stage_c(m + 1)
-        stage_f(m)
-        if m + 1 < M:
-            stage_d(m + 1)
-        stage_g(m)
-        if m + 1 < M:
-            stage_e(m + 1)
-    for m in range(M):
-        stage_h(m)
-    for m in range(M):
+        for one in store(m):
+            one.wait()
         for d in range(1, NY):
             y_in(m, d).wait_send()
             y_out_copy(m, d).wait_send()
@@ -265,14 +285,15 @@
 
 def shards(queries, keys, values, grad_out):
     tokens = queries.shape[0]
-    whole = pl.BlockSpec(memory_space=pltpu.VMEM)
+    whole = pl.BlockSpec(memory_space=pl.ANY)
     dma = pltpu.SemaphoreType.DMA
     return pl.pallas_call(
         kernel,
         out_shape=[jax.ShapeDtypeStruct((tokens, H * DH), BF16)] * 3,
         in_specs=[whole] * 4,
         out_specs=[whole] * 3,
-        scratch_shapes=[
+        scratch_shapes=[pltpu.VMEM((tokens, H * DH), BF16)] * 7
+        + [
             pltpu.VMEM((M, NY, 2, R, DH), BF16),
             pltpu.VMEM((M, NY, 2, R, DH), BF16),
             pltpu.VMEM((M, R, DH), F32),
@@ -290,6 +311,7 @@
             pltpu.VMEM((tokens, H * DH), F32),
             pltpu.VMEM((tokens, H * DH), F32),
             pltpu.VMEM((tokens, H * DH), F32),
+            dma((M, 4)), dma((M, 3)),
             dma((M, NY)), dma((M, NY)),
             dma((M,)), dma((M,)),
             dma((M, NX)), dma((M, NX)),

time: 106 us -> 70.8 us (0.67)
  Pallas kernels: 99.9 us -> 64.7 us
    pallas_call x1, Pallas kernels: 99.9 us -> 64.7 us  [shards(): pl.pallas_call(kernel, out_shape=[jax.ShapeDtypeStruct((tokens, H * DH),...]
where the time goes in v2:
time: 70.8 us; the launch traced here: 70.7 us
  Pallas kernels  64.7 us (91%)
  local copies, waits for them, and re-layouts  5.35 us (8%)
    pallas_call x1, Pallas kernels, shards(): pl.pallas_call(kernel, out_shape=[jax.ShapeDtypeStruct((tokens, H * DH),...  64.7 us
    unnamed x7, local copies, waits for them, and re-layouts  5.35 us

profile of v2, /device:TPU:1, one launch (start us, length us, event | category | flops | bytes accessed | tf_op | source)
XLA Modules:
  0.0 70.7 jit_solution(10175041825498030832)
XLA Ops:
  0.6 0.0 copy-start
  0.6 1.2 %copy-done = bf16[128,4096]{1,0:T(8,128)(2,1)S(1)} copy-done((bf16[128,4096]{1,0:T(8,128)(2,1)S(1)}, bf16[128,4096]{1,0:T(8,128)(2,1)}, u32[]{:S(2)}) %copy-start) | copy-done | bytes 1048600
  1.9 0.0 copy-start.1
  1.9 1.2 %copy-done.1 = bf16[128,4096]{1,0:T(8,128)(2,1)S(1)} copy-done((bf16[128,4096]{1,0:T(8,128)(2,1)S(1)}, bf16[128,4096]{1,0:T(8,128)(2,1)}, u32[]{:S(2)}) %copy-start.1) | copy-done | bytes 1048600
  3.1 64.7 %scan.1 = (bf16[128,4096]{1,0:T(8,128)(2,1)S(1)}, bf16[128,4096]{1,0:T(8,128)(2,1)S(1)}, bf16[128,4096]{1,0:T(8,128)(2,1)S(1)}) custom-call(bf16[128,4096]{1,0:T(8,128)(2,1)S(1)} %copy-done, bf16[128,4096]{1,0:T(8,128)(2,1)S(1)} %copy-done.1, bf16[128,4096]{1,0:T(8,128)(2,1)} %v_hbm.1, bf16[128,4096]{1,0:T(8,128)(2,1)} %g_hbm.1), custom_call_target="tpu_custom_call" | custom-call | flops 1342177280 | bytes 7340032 | tf_op jit(solution)/shard_map/scan/pallas_call | solution.py:290
  67.7 1.0 %copy.10 = bf16[128,4096]{1,0:T(8,128)(2,1)} copy(bf16[128,4096]{1,0:T(8,128)(2,1)S(1)} %get-tuple-element.6) | data formatting | bytes 2097152
  68.7 1.0 %copy.11 = bf16[128,4096]{1,0:T(8,128)(2,1)} copy(bf16[128,4096]{1,0:T(8,128)(2,1)S(1)} %get-tuple-element.7) | data formatting | bytes 2097152
  69.7 1.0 %copy.12 = bf16[128,4096]{1,0:T(8,128)(2,1)} copy(bf16[128,4096]{1,0:T(8,128)(2,1)S(1)} %get-tuple-element.8) | data formatting | bytes 2097152
Async XLA Ops:
  0.6 1.2 %copy-start = (bf16[128,4096]{1,0:T(8,128)(2,1)S(1)}, bf16[128,4096]{1,0:T(8,128)(2,1)}, u32[]{:S(2)}) copy-start(bf16[128,4096]{1,0:T(8,128)(2,1)} %q_hbm.1) | copy-start | bytes 3145732
  1.9 1.2 %copy-start.1 = (bf16[128,4096]{1,0:T(8,128)(2,1)S(1)}, bf16[128,4096]{1,0:T(8,128)(2,1)}, u32[]{:S(2)}) copy-start(bf16[128,4096]{1,0:T(8,128)(2,1)} %k_hbm.1) | copy-start | bytes 3145732

commit v3 on v2

--- a/solution.py
+++ b/solution.py
@@ -321,7 +321,7 @@
             dma((M, NY)), dma((M, NY)),
         ],
         compiler_params=pltpu.CompilerParams(
-            collective_id=0, has_side_effects=True, vmem_limit_bytes=48 * 2**20
+            collective_id=0, has_side_effects=True, vmem_limit_bytes=63 * 2**20
         ),
         cost_estimate=pl.CostEstimate(
             flops=20 * DH**3 * H, bytes_accessed=14 * tokens * H * DH, transcendentals=0

time: 70.8 us -> 71.4 us (level)
  Pallas kernels: 64.7 us -> 65.6 us
    pallas_call x1, Pallas kernels: 64.7 us -> 65.6 us  [shards(): pl.pallas_call(kernel, out_shape=[jax.ShapeDtypeStruct((tokens, H * DH),...]
where the time goes in v3:
time: 71.4 us; the launch traced here: 71.2 us
  Pallas kernels  65.6 us (92%)
  local copies, waits for them, and re-layouts  4.95 us (7%)
    pallas_call x1, Pallas kernels, shards(): pl.pallas_call(kernel, out_shape=[jax.ShapeDtypeStruct((tokens, H * DH),...  65.6 us
    unnamed x7, local copies, waits for them, and re-layouts  4.95 us

profile of v3, /device:TPU:1, one launch (start us, length us, event | category | flops | bytes accessed | tf_op | source)
XLA Modules:
  0.0 71.2 jit_solution(8345876110910031490)
XLA Ops:
  0.6 65.6 %scan.1 = (bf16[128,4096]{1,0:T(8,128)(2,1)}, bf16[128,4096]{1,0:T(8,128)(2,1)}, bf16[128,4096]{1,0:T(8,128)(2,1)}) custom-call(bf16[128,4096]{1,0:T(8,128)(2,1)} %q_hbm.1, bf16[128,4096]{1,0:T(8,128)(2,1)} %k_hbm.1, bf16[128,4096]{1,0:T(8,128)(2,1)} %v_hbm.1, bf16[128,4096]{1,0:T(8,128)(2,1)} %g_hbm.1), custom_call_target="tpu_custom_call" | custom-call | flops 1342177280 | bytes 7340032 | tf_op jit(solution)/shard_map/scan/pallas_call | solution.py:290
  66.3 0.0 copy-start.1
  66.3 2.4 %copy.10 = bf16[128,4096]{1,0:T(8,128)(2,1)} copy(bf16[128,4096]{1,0:T(8,128)(2,1)} %get-tuple-element.6) | data formatting | bytes 2097152
  68.6 0.0 copy-done.1
  68.7 0.0 copy-start
  68.7 1.0 %copy.11 = bf16[128,4096]{1,0:T(8,128)(2,1)} copy(bf16[128,4096]{1,0:T(8,128)(2,1)S(1)} %copy-done.1) | data formatting | bytes 2097152
  69.6 0.6 copy-done
  70.3 1.0 %copy.12 = bf16[128,4096]{1,0:T(8,128)(2,1)} copy(bf16[128,4096]{1,0:T(8,128)(2,1)S(1)} %copy-done) | data formatting | bytes 2097152
Async XLA Ops:
  66.3 2.4 %copy-start.1 = (bf16[128,4096]{1,0:T(8,128)(2,1)S(1)}, bf16[128,4096]{1,0:T(8,128)(2,1)}, u32[]{:S(2)}) copy-start(bf16[128,4096]{1,0:T(8,128)(2,1)} %get-tuple-element.7) | copy-start | bytes 3145732
  68.7 1.6 %copy-start = (bf16[128,4096]{1,0:T(8,128)(2,1)S(1)}, bf16[128,4096]{1,0:T(8,128)(2,1)}, u32[]{:S(2)}) copy-start(bf16[128,4096]{1,0:T(8,128)(2,1)} %get-tuple-element.8) | copy-start | bytes 3145732

commit v4 on v3

--- a/solution.py
+++ b/solution.py
@@ -15,6 +15,9 @@
 R = HC * DH
 RX = R // NX
 UNROLL = 4
+VMEM_MIB = 50
+SPREAD = 1.0
+Y_TIME = 23.0
 MESH = pl.DeviceIdType.MESH
 F32 = jnp.float32
 BF16 = jnp.bfloat16
@@ -28,7 +31,7 @@
 
 def kernel(
     q_hbm, k_hbm, v_hbm, g_hbm, oq_hbm, ok_hbm, ov_hbm,
-    q_ref, k_ref, v_ref, g_ref, oq_ref, ok_ref, ov_ref, sent, got, own_total, other_total, core_out, x_out, x_in, z_buf, x_back, base, base_out, base_other,
+    q_ref, k_ref, v_ref, g_ref, oq_ref, ok_ref, ov_ref, sent, got, own_total, other_total, core_out, x_out, x_in, z_buf, z_sum, x_back, base, base_out, base_other,
     y_out, final, part_q, part_k, part_v,
     in_sem, out_sem, yi_s, yi_r, c1_s, c1_r, xi_s, xi_r, zz_s, zz_r, xo_s, xo_r, c2_s, c2_r, yo_s, yo_r,
 ):
@@ -39,6 +42,7 @@
     z = s // (2 * NX)
     forward = c == 0
     mate = (s + 1 - 2 * c, y)
+    rank = jnp.where(forward, z, NZ - 1 - z)
 
     def at_y(d):
         return lax.rem(y + d, NY)
@@ -46,14 +50,11 @@
     def at_x(d):
         return lax.rem(x + d, NX)
 
-    def at_z(d):
-        return lax.rem(z + d, NZ)
-
     def x_dev(i):
         return ((z * NX + i) * 2 + c, y)
 
-    def z_dev(i):
-        return ((i * NX + x) * 2 + c, y)
+    def z_dev(place):
+        return ((jnp.where(forward, place, NZ - 1 - place) * NX + x) * 2 + c, y)
 
     def copy(src, dst, send, recv, device):
         return pltpu.make_async_remote_copy(
@@ -65,7 +66,7 @@
         [mate]
         + [(s, at_y(d)) for d in range(1, NY)]
         + [x_dev(at_x(d)) for d in range(1, NX)]
-        + [z_dev(at_z(d)) for d in range(1, NZ)]
+        + [z_dev(lax.rem(rank + d, NZ)) for d in range(1, NZ)]
     )
     for partner in partners:
         pl.semaphore_signal(barrier, inc=1, device_id=partner, device_id_type=MESH)
@@ -105,8 +106,9 @@
         return copy(x_out.at[m, at_x(d)], x_in.at[m, slot], xi_s.at[m, d], xi_r.at[m, d], x_dev(at_x(d)))
 
     def z_copy(m, d, receive=False):
-        slot = at_z(NZ - d) if receive else z
-        return copy(z_buf.at[m, z], z_buf.at[m, slot], zz_s.at[m, d], zz_r.at[m, d], z_dev(at_z(d)))
+        slot = rank - d if receive else rank
+        device = z_dev(lax.rem(rank + d, NZ))
+        return copy(z_buf.at[m, rank], z_buf.at[m, slot], zz_s.at[m, d], zz_r.at[m, d], device)
 
     def x_out_copy(m, d, receive=False):
         slot = at_x(NX - d) if receive else x
@@ -187,17 +189,23 @@
         total = x_in[m, 0]
         for i in range(1, NX):
             total += x_in[m, i]
-        z_buf[m, z] = total.astype(BF16)
+        z_buf[m, rank] = total.astype(BF16)
         for d in range(1, NZ):
-            z_copy(m, d).start()
+
+            @pl.when(rank + d < NZ)
+            def _():
+                z_copy(m, d).start()
 
     def stage_z(m):
+        z_sum[m] = jnp.zeros((RX, DH), F32)
         for d in range(1, NZ):
-            z_copy(m, d, True).wait_recv()
-        before = jnp.zeros((RX, DH), F32)
-        for i in range(NZ):
-            wanted = jnp.where(forward, i < z, i > z)
-            before += jnp.where(wanted, z_buf[m, i].astype(F32), 0.0)
+
+            @pl.when(rank - d >= 0)
+            def _():
+                z_copy(m, d, True).wait_recv()
+                z_sum[m] += z_buf[m, rank - d].astype(F32)
+
+        before = z_sum[m]
         ahead = [before]
         behind = [before]
         for i in range(NX - 1):
@@ -258,9 +266,9 @@
 
     steps = []
     for m in range(M):
-        arrives = 23.0 * (m + 1) / M
+        arrives = Y_TIME * (m + 1) / M
         after = ((stage_c, 0), (stage_d, 1.2), (stage_e, 4.2), (stage_z, 9.5), (stage_f, 13), (stage_g, 14))
-        steps += [(arrives + t, m, stage) for stage, t in after]
+        steps += [(arrives + SPREAD * t, m, stage) for stage, t in after]
         steps.append((arrives + 23, m, stage_h))
         steps.append((2.0 + 2.5 * m, m, inside))
     pl.semaphore_wait(barrier, len(partners))
@@ -278,18 +286,32 @@
             x_in_copy(m, d).wait_send()
             x_out_copy(m, d).wait_send()
         for d in range(1, NZ):
-            z_copy(m, d).wait_send()
+
+            @pl.when(rank + d < NZ)
+            def _():
+                z_copy(m, d).wait_send()
+
         core_in(m).wait_send()
         core_out_copy(m).wait_send()
+
+
+def finish(*refs):
+    sources, targets, sem = refs[:3], refs[3:6], refs[6]
+    copies = [pltpu.make_async_copy(a, b, sem.at[n]) for n, (a, b) in enumerate(zip(sources, targets))]
+    for one in copies:
+        one.start()
+    for one in copies:
+        one.wait()
 
 
 def shards(queries, keys, values, grad_out):
     tokens = queries.shape[0]
     whole = pl.BlockSpec(memory_space=pl.ANY)
     dma = pltpu.SemaphoreType.DMA
-    return pl.pallas_call(
+    shapes = [jax.ShapeDtypeStruct((tokens, H * DH), BF16)] * 3
+    results = pl.pallas_call(
         kernel,
-        out_shape=[jax.ShapeDtypeStruct((tokens, H * DH), BF16)] * 3,
+        out_shape=shapes,
         in_specs=[whole] * 4,
         out_specs=[whole] * 3,
         scratch_shapes=[pltpu.VMEM((tokens, H * DH), BF16)] * 7
@@ -302,6 +324,7 @@
             pltpu.VMEM((M, NX, RX, DH), F32),
             pltpu.VMEM((M, NX, RX, DH), F32),
             pltpu.VMEM((M, NZ, RX, DH), BF16),
+            pltpu.VMEM((M, RX, DH), F32),
             pltpu.VMEM((M, NX, RX, DH), F32),
             pltpu.VMEM((M, NX, RX, DH), F32),
             pltpu.VMEM((M, R, DH), F32),
@@ -321,13 +344,22 @@
             dma((M, NY)), dma((M, NY)),
         ],
         compiler_params=pltpu.CompilerParams(
-            collective_id=0, has_side_effects=True, vmem_limit_bytes=63 * 2**20
+            collective_id=0, has_side_effects=True, vmem_limit_bytes=VMEM_MIB * 2**20
         ),
         cost_estimate=pl.CostEstimate(
             flops=20 * DH**3 * H, bytes_accessed=14 * tokens * H * DH, transcendentals=0
         ),
         name="scan",
     )(queries, keys, values, grad_out)
+    return pl.pallas_call(
+        finish,
+        out_shape=shapes,
+        in_specs=[whole] * 3,
+        out_specs=[whole] * 3,
+        scratch_shapes=[dma((3,))],
+        cost_estimate=pl.CostEstimate(flops=0, bytes_accessed=12 * tokens * H * DH, transcendentals=0),
+        name="finish",
+    )(*results)
 
 
 def solution(mesh):

time: 71.4 us -> 162 us (2.27)
  Pallas kernels: 65.6 us -> 158 us
  local copies, waits for them, and re-layouts: 4.95 us -> 2.97 us
    pallas_call x1 -> x2, Pallas kernels: 65.6 us -> 158 us  [the longest x1 96.4 us: shards(): pl.pallas_call(finish, out_shape=shapes, in_specs=[whole] * 3, out_specs=...]
    unnamed x7 -> x6, local copies, waits for them, and re-layouts: 4.95 us -> 2.97 us
where the time goes in v4:
time: 162 us
  Pallas kernels  158 us (98%)
  local copies, waits for them, and re-layouts  2.97 us (2%)
    pallas_call x1, Pallas kernels, shards(): pl.pallas_call(finish, out_shape=shapes, in_specs=[whole] * 3, out_specs=...  96.4 us
    pallas_call x1, Pallas kernels, shards(): pl.pallas_call(kernel, out_shape=shapes, in_specs=[whole] * 4, out_specs=...  62 us

profile of v4, /device:TPU:1, one launch (start us, length us, event | category | flops | bytes accessed | tf_op | source)
XLA Modules:
  0.0 162.1 jit_solution(11880848817017124849)
XLA Ops:
  0.6 62.0 %scan.1 = (bf16[128,4096]{1,0:T(8,128)(2,1)S(1)}, bf16[128,4096]{1,0:T(8,128)(2,1)S(1)}, bf16[128,4096]{1,0:T(8,128)(2,1)S(1)}) custom-call(bf16[128,4096]{1,0:T(8,128)(2,1)} %q_hbm.1, bf16[128,4096]{1,0:T(8,128)(2,1)} %k_hbm.1, bf16[128,4096]{1,0:T(8,128)(2,1)} %v_hbm.1, bf16[128,4096]{1,0:T(8,128)(2,1)} %g_hbm.1), custom_call_target="tpu_custom_call" | custom-call | flops 1342177280 | bytes 7340032 | tf_op jit(solution)/shard_map/scan/pallas_call | solution.py:312
  62.7 0.0 copy-start
  62.7 1.0 copy-done
  63.6 0.0 copy-start.1
  63.6 1.0 copy-done.1
  64.6 0.0 copy-start.2
  64.6 1.0 copy-done.2
  65.6 96.4 %finish.1 = (bf16[128,4096]{1,0:T(8,128)(2,1)}, bf16[128,4096]{1,0:T(8,128)(2,1)}, bf16[128,4096]{1,0:T(8,128)(2,1)}) custom-call(bf16[128,4096]{1,0:T(8,128)(2,1)} %copy-done, bf16[128,4096]{1,0:T(8,128)(2,1)} %copy-done.1, bf16[128,4096]{1,0:T(8,128)(2,1)} %copy-done.2), custom_call_target="tpu_custom_call" | custom-call | bytes 6291456 | tf_op jit(solution)/shard_map/finish/pallas_call | solution.py:354
Async XLA Ops:
  62.7 1.0 copy-start
  63.6 1.0 copy-start.1
  64.6 1.0 copy-start.2

commit v5 on v4

--- a/solution.py
+++ b/solution.py
@@ -309,7 +309,7 @@
     whole = pl.BlockSpec(memory_space=pl.ANY)
     dma = pltpu.SemaphoreType.DMA
     shapes = [jax.ShapeDtypeStruct((tokens, H * DH), BF16)] * 3
-    results = pl.pallas_call(
+    return pl.pallas_call(
         kernel,
         out_shape=shapes,
         in_specs=[whole] * 4,
@@ -351,16 +351,6 @@
         ),
         name="scan",
     )(queries, keys, values, grad_out)
-    return pl.pallas_call(
-        finish,
-        out_shape=shapes,
-        in_specs=[whole] * 3,
-        out_specs=[whole] * 3,
-        scratch_shapes=[dma((3,))],
-        cost_estimate=pl.CostEstimate(flops=0, bytes_accessed=12 * tokens * H * DH, transcendentals=0),
-        name="finish",
-    )(*results)
-
 
 def solution(mesh):
     spec = P(("seq", "head"), None)

time: 162 us -> 65.7 us (0.41)
  Pallas kernels: 158 us -> 62 us
    pallas_call x1 -> x0, Pallas kernels: 96.4 us -> none  [shards(): pl.pallas_call(finish, out_shape=shapes, in_specs=[whole] * 3, out_specs=...]
where the time goes in v5:
time: 65.7 us; the launch traced here: 65.6 us
  Pallas kernels  62 us (94%)
  local copies, waits for them, and re-layouts  2.91 us (4%)
    pallas_call x1, Pallas kernels, shards(): pl.pallas_call(kernel, out_shape=shapes, in_specs=[whole] * 4, out_specs=...  62 us
    unnamed x3, local copies, waits for them, and re-layouts  2.91 us

profile of v5, /device:TPU:1, one launch (start us, length us, event | category | flops | bytes accessed | tf_op | source)
XLA Modules:
  0.0 65.6 jit_solution(11081463183258429297)
XLA Ops:
  0.6 62.0 %scan.1 = (bf16[128,4096]{1,0:T(8,128)(2,1)S(1)}, bf16[128,4096]{1,0:T(8,128)(2,1)S(1)}, bf16[128,4096]{1,0:T(8,128)(2,1)S(1)}) custom-call(bf16[128,4096]{1,0:T(8,128)(2,1)} %q_hbm.1, bf16[128,4096]{1,0:T(8,128)(2,1)} %k_hbm.1, bf16[128,4096]{1,0:T(8,128)(2,1)} %v_hbm.1, bf16[128,4096]{1,0:T(8,128)(2,1)} %g_hbm.1), custom_call_target="tpu_custom_call" | custom-call | flops 1342177280 | bytes 7340032 | tf_op jit(solution)/shard_map/scan/pallas_call | solution.py:312
  62.7 1.0 %copy.10 = bf16[128,4096]{1,0:T(8,128)(2,1)} copy(bf16[128,4096]{1,0:T(8,128)(2,1)S(1)} %get-tuple-element.6) | data formatting | bytes 2097152
  63.6 1.0 %copy.11 = bf16[128,4096]{1,0:T(8,128)(2,1)} copy(bf16[128,4096]{1,0:T(8,128)(2,1)S(1)} %get-tuple-element.7) | data formatting | bytes 2097152
  64.6 1.0 %copy.12 = bf16[128,4096]{1,0:T(8,128)(2,1)} copy(bf16[128,4096]{1,0:T(8,128)(2,1)S(1)} %get-tuple-element.8) | data formatting | bytes 2097152

commit v6 on v4

--- a/solution.py
+++ b/solution.py
@@ -30,10 +30,10 @@
 
 
 def kernel(
-    q_hbm, k_hbm, v_hbm, g_hbm, oq_hbm, ok_hbm, ov_hbm,
-    q_ref, k_ref, v_ref, g_ref, oq_ref, ok_ref, ov_ref, sent, got, own_total, other_total, core_out, x_out, x_in, z_buf, z_sum, x_back, base, base_out, base_other,
+    q_hbm, k_hbm, v_hbm, g_hbm, oq_ref, ok_ref, ov_ref,
+    q_ref, k_ref, v_ref, g_ref, sent, got, own_total, other_total, core_out, x_out, x_in, z_buf, z_sum, x_back, base, base_out, base_other,
     y_out, final, part_q, part_k, part_v,
-    in_sem, out_sem, yi_s, yi_r, c1_s, c1_r, xi_s, xi_r, zz_s, zz_r, xo_s, xo_r, c2_s, c2_r, yo_s, yo_r,
+    in_sem, yi_s, yi_r, c1_s, c1_r, xi_s, xi_r, zz_s, zz_r, xo_s, xo_r, c2_s, c2_r, yo_s, yo_r,
 ):
     s = lax.axis_index("seq")
     y = lax.axis_index("head")
@@ -79,14 +79,6 @@
         pairs = ((k_hbm, k_ref), (v_hbm, v_ref), (q_hbm, q_ref), (g_hbm, g_ref))
         return [
             pltpu.make_async_copy(a.at[:, columns], b.at[:, columns], in_sem.at[m, n])
-            for n, (a, b) in enumerate(pairs)
-        ]
-
-    def store(m):
-        columns = slice(m * WIDE, (m + 1) * WIDE)
-        pairs = ((oq_ref, oq_hbm), (ok_ref, ok_hbm), (ov_ref, ov_hbm))
-        return [
-            pltpu.make_async_copy(a.at[:, columns], b.at[:, columns], out_sem.at[m, n])
             for n, (a, b) in enumerate(pairs)
         ]
 
@@ -261,8 +253,6 @@
                 ok_ref[:, at] = (part_k[:, at] + dot(v_ref[:, at], suffix, 1, 1)).astype(BF16)
                 ov_ref[:, at] = (part_v[:, at] + dot(k_ref[:, at], suffix, 1, 0)).astype(BF16)
 
-        for one in store(m):
-            one.start()
 
     steps = []
     for m in range(M):
@@ -277,8 +267,6 @@
     for _, m, stage in sorted(steps, key=lambda step: step[:2]):
         stage(m)
     for m in range(M):
-        for one in store(m):
-            one.wait()
         for d in range(1, NY):
             y_in(m, d).wait_send()
             y_out_copy(m, d).wait_send()
@@ -313,8 +301,8 @@
         kernel,
         out_shape=shapes,
         in_specs=[whole] * 4,
-        out_specs=[whole] * 3,
-        scratch_shapes=[pltpu.VMEM((tokens, H * DH), BF16)] * 7
+        out_specs=[pl.BlockSpec(memory_space=pltpu.VMEM)] * 3,
+        scratch_shapes=[pltpu.VMEM((tokens, H * DH), BF16)] * 4
         + [
             pltpu.VMEM((M, NY, 2, R, DH), BF16),
             pltpu.VMEM((M, NY, 2, R, DH), BF16),
@@ -334,7 +322,7 @@
             pltpu.VMEM((tokens, H * DH), F32),
             pltpu.VMEM((tokens, H * DH), F32),
             pltpu.VMEM((tokens, H * DH), F32),
-            dma((M, 4)), dma((M, 3)),
+            dma((M, 4)),
             dma((M, NY)), dma((M, NY)),
             dma((M,)), dma((M,)),
             dma((M, NX)), dma((M, NX)),
@@ -354,10 +342,11 @@
     return pl.pallas_call(
         finish,
         out_shape=shapes,
-        in_specs=[whole] * 3,
+        in_specs=[pl.BlockSpec(memory_space=pltpu.VMEM)] * 3,
         out_specs=[whole] * 3,
         scratch_shapes=[dma((3,))],
         cost_estimate=pl.CostEstimate(flops=0, bytes_accessed=12 * tokens * H * DH, transcendentals=0),
+        compiler_params=pltpu.CompilerParams(vmem_limit_bytes=8 * 2**20),
         name="finish",
     )(*results)
 

time: 162 us -> 64.3 us (0.40)
  Pallas kernels: 158 us -> 63.5 us
  local copies, waits for them, and re-layouts: 2.97 us -> 0 us
    pallas_call x1, Pallas kernels: 96.4 us -> 1.69 us  [shards(): pl.pallas_call(finish, out_shape=shapes, in_specs=[pl.BlockSpec(memory_sp...]
    unnamed x6 -> x0, local copies, waits for them, and re-layouts: 2.97 us -> none
where the time goes in v6:
time: 64.3 us; the launch traced here: 64.2 us
  Pallas kernels  63.5 us (99%)
    pallas_call x1, Pallas kernels, shards(): pl.pallas_call(kernel, out_shape=shapes, in_specs=[whole] * 4, out_specs=...  61.8 us
    pallas_call x1, Pallas kernels, shards(): pl.pallas_call(finish, out_shape=shapes, in_specs=[pl.BlockSpec(memory_sp...  1.69 us

profile of v6, /device:TPU:1, one launch (start us, length us, event | category | flops | bytes accessed | tf_op | source)
XLA Modules:
  0.0 64.2 jit_solution(8936447232747259368)
XLA Ops:
  0.6 61.8 %scan.1 = (bf16[128,4096]{1,0:T(8,128)(2,1)S(1)}, bf16[128,4096]{1,0:T(8,128)(2,1)S(1)}, bf16[128,4096]{1,0:T(8,128)(2,1)S(1)}) custom-call(bf16[128,4096]{1,0:T(8,128)(2,1)} %q_hbm.1, bf16[128,4096]{1,0:T(8,128)(2,1)} %k_hbm.1, bf16[128,4096]{1,0:T(8,128)(2,1)} %v_hbm.1, bf16[128,4096]{1,0:T(8,128)(2,1)} %g_hbm.1), custom_call_target="tpu_custom_call" | custom-call | flops 1342177280 | bytes 7340032 | tf_op jit(solution)/shard_map/scan/pallas_call | solution.py:300
  62.5 1.7 %finish.1 = (bf16[128,4096]{1,0:T(8,128)(2,1)}, bf16[128,4096]{1,0:T(8,128)(2,1)}, bf16[128,4096]{1,0:T(8,128)(2,1)}) custom-call(bf16[128,4096]{1,0:T(8,128)(2,1)S(1)} %get-tuple-element.6.refs_0_, bf16[128,4096]{1,0:T(8,128)(2,1)S(1)} %get-tuple-element.7.refs_1_, bf16[128,4096]{1,0:T(8,128)(2,1)S(1)} %get-tuple-element.8.refs_2_), custom_call_target="tpu_custom_call" | custom-call | bytes 6291456 | tf_op jit(solution)/shard_map/finish/pallas_call | solution.py:342

commit v7 on v6

--- a/solution.py
+++ b/solution.py
@@ -14,7 +14,7 @@
 WIDE = NY * HC * DH
 R = HC * DH
 RX = R // NX
-UNROLL = 4
+UNROLL = 8
 VMEM_MIB = 50
 SPREAD = 1.0
 Y_TIME = 23.0

time: 64.3 us -> 63.9 us (level)
  no operation moved by 1% of the time
where the time goes in v7:
time: 63.9 us; the launch traced here: 63.8 us
  Pallas kernels  63.2 us (99%)
  between operations  0.64 us (1%)
    pallas_call x1, Pallas kernels, shards(): pl.pallas_call(kernel, out_shape=shapes, in_specs=[whole] * 4, out_specs=...  61.5 us
    pallas_call x1, Pallas kernels, shards(): pl.pallas_call(finish, out_shape=shapes, in_specs=[pl.BlockSpec(memory_sp...  1.69 us

profile of v7, /device:TPU:1, one launch (start us, length us, event | category | flops | bytes accessed | tf_op | source)
XLA Modules:
  0.0 63.8 jit_solution(22412467473375367)
XLA Ops:
  0.6 61.5 %scan.1 = (bf16[128,4096]{1,0:T(8,128)(2,1)S(1)}, bf16[128,4096]{1,0:T(8,128)(2,1)S(1)}, bf16[128,4096]{1,0:T(8,128)(2,1)S(1)}) custom-call(bf16[128,4096]{1,0:T(8,128)(2,1)} %q_hbm.1, bf16[128,4096]{1,0:T(8,128)(2,1)} %k_hbm.1, bf16[128,4096]{1,0:T(8,128)(2,1)} %v_hbm.1, bf16[128,4096]{1,0:T(8,128)(2,1)} %g_hbm.1), custom_call_target="tpu_custom_call" | custom-call | flops 1342177280 | bytes 7340032 | tf_op jit(solution)/shard_map/scan/pallas_call | solution.py:300
  62.1 1.7 %finish.1 = (bf16[128,4096]{1,0:T(8,128)(2,1)}, bf16[128,4096]{1,0:T(8,128)(2,1)}, bf16[128,4096]{1,0:T(8,128)(2,1)}) custom-call(bf16[128,4096]{1,0:T(8,128)(2,1)S(1)} %get-tuple-element.6.refs_0_, bf16[128,4096]{1,0:T(8,128)(2,1)S(1)} %get-tuple-element.7.refs_1_, bf16[128,4096]{1,0:T(8,128)(2,1)S(1)} %get-tuple-element.8.refs_2_), custom_call_target="tpu_custom_call" | custom-call | bytes 6291456 | tf_op jit(solution)/shard_map/finish/pallas_call | solution.py:342
